TPU v7x, 32 devices: a whole 2x2x4 slice. The times are simulated.
32 devices in a mesh: shot: 4 (over x, core), rcv: 8 (over z, y).
Axes of the slice: x: 2, y: 2, z: 4, core: 2. Of those that a mesh axis runs over, the one named last changes fastest.
Arguments:
- data: float32 [1, 2, 8192, 1024], P(None, None, 'rcv', 'shot'), may hold values from -6 to 6
- impulse: float32 [1, 2, 8192, 8192], P(None, None, 'rcv'), may hold values from -0.0625 to 0.0625
- wavelet: float32 [1, 2], replicated, may hold values from -96 to 96
- live: int32 [8192, 1024], P('rcv', 'shot'), may hold values from 0 to 1, as said below
Outputs:
- residual: float32 [1, 2, 8192, 1024], P(None, None, 'rcv', 'shot')
- gradient: float32 [1, 2, 8192, 8192], P(None, None, 'rcv', 'shot')
Inputs may be any that keep to these rules, and one draw needn't show every extreme that they name: live[r, s] is 0 where |r - s * 8| is at most a per-shot half gap of 1 to 4 positions, and at scattered dead traces; 1 elsewhere.
All inputs are finite; a program needn't handle non-finite values.
Results may differ from a plain program's by a relative error of at most 0.000084.
Values sent between devices are 32-bit elements; how exact they have to be, the bound alone decides.
A program may use at most 320 MiB of HBM per device.

v0:
```python
import jax
import jax.numpy as jnp
from jax import lax
from jax.sharding import PartitionSpec as P


def product(left, right, form):
    return jnp.einsum(
        form, left, right, precision=lax.Precision.HIGHEST, preferred_element_type=jnp.float32
    )


def convolve(impulse_cols, panel):
    left_re = impulse_cols[:, 0]
    left_im = impulse_cols[:, 1]
    right_re = panel[:, 0]
    right_im = panel[:, 1]
    out_re = product(left_re, right_re, "frk,fks->frs") - product(left_im, right_im, "frk,fks->frs")
    out_im = product(left_re, right_im, "frk,fks->frs") + product(left_im, right_re, "frk,fks->frs")
    return jnp.stack([out_re, out_im], axis=1)


def correlate(residual, panel, scale):
    res_re = residual[:, 0]
    res_im = residual[:, 1]
    pan_re = panel[:, 0]
    pan_im = panel[:, 1]
    out_re = product(res_re, pan_re, "frs,fks->frk") + product(res_im, pan_im, "frs,fks->frk")
    out_im = product(res_im, pan_re, "frs,fks->frk") - product(res_re, pan_im, "frs,fks->frk")
    return jnp.stack([out_re, out_im], axis=1) * scale


def local(data, impulse, wavelet, live):
    rows_dev = data.shape[2]
    shots_dev = data.shape[3]
    positions = impulse.shape[3]
    total_shots = shots_dev * lax.axis_size("shot")
    spacing = positions // total_shots
    scale = -(total_shots ** (-0.5))
    mask = live.astype(jnp.float32)
    observed = data * mask[None, None]
    row_ids = lax.axis_index("rcv") * rows_dev + lax.broadcasted_iota(
        jnp.int32, (rows_dev, shots_dev), 0
    )
    col_ids = lax.axis_index("shot") * shots_dev + lax.broadcasted_iota(
        jnp.int32, (rows_dev, shots_dev), 1
    )
    source = (row_ids == col_ids * spacing).astype(jnp.float32)
    panel = wavelet[:, :, None, None] * source[None, None] - observed
    predicted = convolve(impulse, lax.all_gather(panel, "rcv", axis=2, tiled=True))
    residual = mask[None, None] * (observed - predicted)
    terms = correlate(residual, lax.all_gather(panel, "rcv", axis=2, tiled=True), scale)
    gradient = lax.psum_scatter(terms, "shot", scatter_dimension=3, tiled=True)
    return (residual, gradient)


def solution(mesh):
    placed = (P(None, None, "rcv", "shot"), P(None, None, "rcv", None), P(), P("rcv", "shot"))
    return jax.shard_map(
        local,
        mesh=mesh,
        in_specs=placed,
        out_specs=(P(None, None, "rcv", "shot"), P(None, None, "rcv", "shot")),
        check_vma=False,
    )
```

profile of v0, /device:TPU:0, one launch (start us, length us, event | category | flops | bytes accessed | tf_op | source)
XLA Modules:
  0.0 1009.3 jit_solution(9402485186113827683)
XLA Ops:
  7.2 0.0 all-gather.2.cloned.1.call-start
  7.2 1.3 convert_element_type.10
  8.5 0.3 copy.6
  8.9 1.9 copy.7
  10.8 0.0 copy-start.1
  10.8 0.1 compare_convert_fusion
  11.0 2.6 multiply_subtract_fusion
  13.5 0.0 all-gather.2.cloned.1.call-update
  13.6 0.0 reduce-scatter.2.cloned.1.call-start
  13.6 230.4 %all-gather.2.cloned.1.call-done = f32[1,2,8192,256]{2,3,1,0:T(8,128)} async-done(((f32[1,2,1024,256]{2,3,1,0:T(8,128)}), f32[1,2,8192,256]{2,3,1,0:T(8,128)}) %all-gather.2.cloned.1.call-update) | async-done | bytes 16777232 | tf_op jit(solution)/shard_map/all_gather | solution.py:50
  244.0 32.4 %fusion = f32[256,1024]{1,0:T(8,128)S(1)} fusion(f32[1,2,1024,8192]{3,2,1,0:T(8,128)} %param.5, f32[1,2,8192,256]{2,3,1,0:T(8,128)} %all-gather.2.cloned.1.call-done), kind=kOutput, calls=%fused_computation.1 | convolution fusion | flops 25769803776 | bytes 42991616 | tf_op jit(solution)/shard_map/frk,fks->frs/dot_general | solution.py:8
  276.4 31.9 %fusion.2 = f32[256,1024]{1,0:T(8,128)S(1)} fusion(f32[1,2,1024,8192]{3,2,1,0:T(8,128)} %param.5, f32[1,2,8192,256]{2,3,1,0:T(8,128)S(1)} %copy-done), kind=kOutput, calls=%fused_computation.3 | convolution fusion | flops 25769803776 | bytes 42991616 | tf_op jit(solution)/shard_map/frk,fks->frs/dot_general | solution.py:8
  308.4 32.4 %fusion.24 = f32[1,1,1024,256]{2,3,1,0:T(8,128)S(1)} fusion(f32[256,1024]{1,0:T(8,128)S(1)} %fusion, f32[1,2,1024,8192]{3,2,1,0:T(8,128)} %param.5, f32[1,2,8192,256]{2,3,1,0:T(8,128)} %all-gather.2.cloned.1.call-done), kind=kOutput, calls=%fused_computation.25 | convolution fusion | flops 25770065920 | bytes 44040192 | tf_op jit(solution)/shard_map/frk,fks->frs/dot_general | solution.py:8
  340.8 0.0 copy-start.2
  340.8 32.7 %fusion.18 = f32[1,1,1024,256]{2,3,1,0:T(8,128)S(1)} fusion(f32[256,1024]{1,0:T(8,128)S(1)} %fusion.2, f32[1,2,1024,8192]{3,2,1,0:T(8,128)} %param.5, f32[1,2,8192,256]{2,3,1,0:T(8,128)} %all-gather.2.cloned.1.call-done), kind=kOutput, calls=%fused_computation.23 | convolution fusion | flops 25770065920 | bytes 44040192 | tf_op jit(solution)/shard_map/frk,fks->frs/dot_general | solution.py:8
  373.5 0.6 fusion.14
  374.1 32.2 %fusion.12 = f32[1024,8192]{1,0:T(8,128)} fusion(f32[1,2,8192,256]{2,3,1,0:T(8,128)} %all-gather.2.cloned.1.call-done, f32[1,2,1024,256]{2,3,1,0:T(8,128)S(1)} %fusion.14), kind=kOutput, calls=%fused_computation.17 | convolution fusion | flops 25769803776 | bytes 42991616 | tf_op jit(solution)/shard_map/frs,fks->frk/dot_general | solution.py:8
  406.4 30.8 %fusion.13 = f32[1024,8192]{1,0:T(8,128)} fusion(f32[1,2,8192,256]{2,3,1,0:T(8,128)S(1)} %bitcast.60, f32[1,2,1024,256]{2,3,1,0:T(8,128)S(1)} %fusion.14), kind=kOutput, calls=%fused_computation.18 | convolution fusion | flops 25769803776 | bytes 42991616 | tf_op jit(solution)/shard_map/frs,fks->frk/dot_general | solution.py:8
  437.3 34.9 %subtract_bitcast_fusion = f32[1,1,1024,8192]{3,2,1,0:T(8,128)} fusion(f32[1024,8192]{1,0:T(8,128)} %fusion.12, f32[1,2,8192,256]{2,3,1,0:T(8,128)} %all-gather.2.cloned.1.call-done, f32[1,2,1024,256]{2,3,1,0:T(8,128)S(1)} %fusion.14), kind=kOutput, calls=%fused_computation.9 | convolution fusion | flops 25778192384 | bytes 76546048 | tf_op jit(solution)/shard_map/frs,fks->frk/dot_general | solution.py:8
  472.2 35.0 %add_bitcast_fusion = f32[1,1,1024,8192]{3,2,1,0:T(8,128)} fusion(f32[1024,8192]{1,0:T(8,128)} %fusion.13, f32[1,2,8192,256]{2,3,1,0:T(8,128)} %all-gather.2.cloned.1.call-done, f32[1,2,1024,256]{2,3,1,0:T(8,128)S(1)} %fusion.14), kind=kOutput, calls=%fused_computation.10 | convolution fusion | flops 25778192384 | bytes 76546048 | tf_op jit(solution)/shard_map/frs,fks->frk/dot_general | solution.py:8
  507.2 44.4 %maximum_multiply_fusion = f32[1,2,1024,8192]{3,2,1,0:T(8,128)} fusion(f32[1,1,1024,8192]{3,2,1,0:T(8,128)} %subtract_bitcast_fusion, f32[1,1,1024,8192]{3,2,1,0:T(8,128)} %add_bitcast_fusion), kind=kLoop, calls=%fused_computation | loop fusion | flops 33554432 | bytes 134217728 | tf_op jit(solution)/shard_map/mul | solution.py:30
  551.5 0.0 reduce-scatter.2.cloned.1.call-update
  551.6 1.8 copy.8
  553.4 448.8 %reduce-scatter.2.cloned.1.call-done = f32[1,2,1024,2048]{3,2,1,0:T(8,128)} async-done(((f32[1,2,1024,8192]{3,2,1,0:T(8,128)}), f32[1,2,1024,2048]{3,2,1,0:T(8,128)}) %reduce-scatter.2.cloned.1.call-update) | async-done | bytes 16777232 | tf_op jit(solution)/shard_map/reduce_scatter | solution.py:53
  (15 shorter events, 0.0 us)
Async XLA Ops:
  7.2 236.8 %all-gather.2.cloned.1.call-start = ((), (), s32[]{:S(2)}) async-start(), calls=%async_computation.1 | async-start | bytes 18874368 | tf_op jit(solution)/shard_map/all_gather | solution.py:50
  10.8 265.6 %copy-start.1 = (f32[1,2,1024,256]{2,3,1,0:T(8,128)}, f32[1,2,1024,256]{2,3,1,0:T(8,128)S(1)}, u32[]{:S(2)}) copy-start(f32[1,2,1024,256]{2,3,1,0:T(8,128)S(1)} %copy.7) | copy-start | bytes 6291460
  13.6 988.6 %reduce-scatter.2.cloned.1.call-start = ((), (), s32[]{:S(2)}) async-start(), calls=%async_computation.2 | async-start | bytes 83886080 | tf_op jit(solution)/shard_map/reduce_scatter | solution.py:53
  244.0 32.4 %copy-start = (f32[1,2,8192,256]{2,3,1,0:T(8,128)S(1)}, f32[1,2,8192,256]{2,3,1,0:T(8,128)}, u32[]{:S(2)}) copy-start(f32[1,2,8192,256]{2,3,1,0:T(8,128)} %all-gather.2.cloned.1.call-done) | copy-start | bytes 50331652
  340.8 32.8 %copy-start.2 = (f32[1,2,1024,256]{2,3,1,0:T(8,128)S(1)}, f32[1,2,1024,256]{2,3,1,0:T(8,128)}, u32[]{:S(2)}) copy-start(f32[1,2,1024,256]{2,3,1,0:T(8,128)} %copy-done.1) | copy-start | bytes 6291460
  373.5 32.9 %slice-start = ((s8[16777216]{0:T(1024)(128)(4,1)}), s8[4194304]{0:T(1024)(128)(4,1)S(1)}, s32[]{:S(2)}) async-start(s8[16777216]{0:T(1024)(128)(4,1)} %bitcast.59), calls=%async_computation.3 | async-start | bytes 8388608
  374.1 32.3 %slice-start.1 = ((s8[16777216]{0:T(1024)(128)(4,1)}), s8[4194304]{0:T(1024)(128)(4,1)S(1)}, s32[]{:S(2)}) async-start(s8[16777216]{0:T(1024)(128)(4,1)} %bitcast.59), calls=%async_computation.4 | async-start | bytes 8388608
  374.1 32.3 %slice-start.2 = ((s8[16777216]{0:T(1024)(128)(4,1)}), s8[4194304]{0:T(1024)(128)(4,1)S(1)}, s32[]{:S(2)}) async-start(s8[16777216]{0:T(1024)(128)(4,1)} %bitcast.59), calls=%async_computation.5 | async-start | bytes 8388608
  374.1 32.3 %slice-start.3 = ((s8[16777216]{0:T(1024)(128)(4,1)}), s8[4194304]{0:T(1024)(128)(4,1)S(1)}, s32[]{:S(2)}) async-start(s8[16777216]{0:T(1024)(128)(4,1)} %bitcast.59), calls=%async_computation.6 | async-start | bytes 8388608
Sparse Core Ops, SparseCore 0:
  13.7 230.2 all-gather.1
  551.7 450.4 reduce-scatter.1
where the time goes:
time: 1020 us; the launch traced here: 1010 us
  waiting for transfers between devices  679 us (67%)
  matrix products  262 us (26%)
  other arithmetic  49 us (5%)
  between operations  14.4 us (1%)
    reduce_scatter x1, waiting for transfers between devices, local(): gradient = lax.psum_scatter(terms, 'shot', scatter_dimension=3, tiled=True)  449 us
    dot_general x8, matrix products, product(): jnp.einsum(form, left, right, precision=lax.Precision.HIGHEST, preferred_...  262 us
    all_gather x1, waiting for transfers between devices, local(): lax.all_gather(panel, 'rcv', axis=2, tiled=True)  230 us
    mul x1, other arithmetic, correlate(): return jnp.stack([out_re, out_im], axis=1) * scale  44.4 us
  transfers between devices with their start and end apart: 2, of which 2 were waited for; matrix products, arithmetic and copies ran while one was open for 0% of the time, Pallas kernels for 0%

commit v1 on v0

v1 whole, which is shorter than its diff:
```python
import functools

import jax
import jax.numpy as jnp
from jax import lax
from jax.experimental import pallas as pl
from jax.experimental.pallas import tpu as pltpu
from jax.sharding import PartitionSpec as P

MESH = pl.DeviceIdType.MESH
PRECISION = lax.Precision.HIGH


def product(left, right, form):
    return jnp.einsum(form, left, right, precision=PRECISION, preferred_element_type=jnp.float32)


def convolve(imp, panel):
    form = "rk,ks->rs"
    out_re = product(imp[0], panel[0], form) - product(imp[1], panel[1], form)
    out_im = product(imp[0], panel[1], form) + product(imp[1], panel[0], form)
    return jnp.stack([out_re, out_im])


def correlate(res, panel, scale):
    form = "rs,ks->rk"
    out_re = product(res[0], panel[0], form) + product(res[1], panel[1], form)
    out_im = product(res[1], panel[0], form) - product(res[0], panel[1], form)
    return jnp.stack([out_re, out_im]) * scale


def spread_kernel(planes, panel_ref, gath_ref, line_recv, y_recv, send_src, send_up, send_down, send_y, local_sem):
    j = lax.axis_index("shot")
    b = lax.axis_index("rcv")
    z, y = b // 2, lax.rem(b, 2)
    other = z * 2 + 1 - y
    rows, shots = panel_ref.shape[1], panel_ref.shape[2]

    barrier = pltpu.get_barrier_semaphore()
    for d in range(1, planes):
        pl.semaphore_signal(barrier, inc=1, device_id=(lax.rem(j + d, planes), b), device_id_type=MESH)
    pl.semaphore_signal(barrier, inc=1, device_id=(j, other), device_id_type=MESH)

    @pl.when(z < planes - 1)
    def _():
        pl.semaphore_signal(barrier, inc=1, device_id=(j, b + 2), device_id_type=MESH)

    @pl.when(z > 0)
    def _():
        pl.semaphore_signal(barrier, inc=1, device_id=(j, b - 2), device_id_type=MESH)

    ends = (z == 0).astype(jnp.int32) + (z == planes - 1).astype(jnp.int32)
    pl.semaphore_wait(barrier, planes + 2 - ends)

    def slot(a, side, p):
        return gath_ref.at[p, pl.ds(pl.multiple_of(side * rows, rows), rows), pl.ds(pl.multiple_of(a * shots, shots), shots)]

    def source(p):
        i = lax.rem(j - z + planes, planes)
        return pltpu.make_async_remote_copy(
            src_ref=panel_ref.at[p], dst_ref=slot(j, y, p), send_sem=send_src.at[p],
            recv_sem=line_recv.at[i * 2 + p], device_id=(z, b), device_id_type=MESH)

    def own(p):
        return pltpu.make_async_copy(panel_ref.at[p], slot(j, y, p), local_sem.at[p])

    @pl.when(j != z)
    def _():
        for p in range(2):
            source(p).start()

    @pl.when(j == z)
    def _():
        for p in range(2):
            own(p).start()

    def step(i, p):
        a = lax.rem(j + i, planes)
        ref = slot(a, y, p)
        n = i * 2 + p

        def to(dev, send, recv):
            return pltpu.make_async_remote_copy(
                src_ref=ref, dst_ref=ref, send_sem=send.at[n], recv_sem=recv.at[n],
                device_id=(j, dev), device_id_type=MESH)

        return n, to

    up_ok = jnp.logical_and(z >= j, z < planes - 1)
    down_ok = jnp.logical_and(z <= j, z > 0)
    for i in range(planes):
        for p in range(2):
            n, to = step(i, p)
            if i == 0:
                @pl.when(j == z)
                def _():
                    own(p).wait()

                @pl.when(j != z)
                def _():
                    to(other, send_y, line_recv).wait_recv()
            else:
                to(other, send_y, line_recv).wait_recv()

            @pl.when(up_ok)
            def _():
                to(b + 2, send_up, line_recv).start()

            @pl.when(down_ok)
            def _():
                to(b - 2, send_down, line_recv).start()

            to(other, send_y, y_recv).start()

    for i in range(planes):
        for p in range(2):
            n, to = step(i, p)

            @pl.when(up_ok)
            def _():
                to(b + 2, send_up, line_recv).wait_send()

            @pl.when(down_ok)
            def _():
                to(b - 2, send_down, line_recv).wait_send()

            to(other, send_y, y_recv).wait_send()
            a = lax.rem(j + i, planes)
            ref = slot(a, 1 - y, p)
            pltpu.make_async_remote_copy(
                src_ref=ref, dst_ref=ref, send_sem=send_y.at[n], recv_sem=y_recv.at[n],
                device_id=(j, other), device_id_type=MESH).wait_recv()

    @pl.when(j != z)
    def _():
        for p in range(2):
            source(p).wait_send()


def spread(panel, planes):
    _, rows, shots = panel.shape
    dma = pltpu.SemaphoreType.DMA
    return pl.pallas_call(
        functools.partial(spread_kernel, planes),
        out_shape=jax.ShapeDtypeStruct((2, 2 * rows, planes * shots), jnp.float32),
        in_specs=[pl.BlockSpec(memory_space=pl.ANY)],
        out_specs=pl.BlockSpec(memory_space=pl.ANY),
        scratch_shapes=[dma((2 * planes,)), dma((2 * planes,)), dma((2,)), dma((2 * planes,)),
                        dma((2 * planes,)), dma((2 * planes,)), dma((2,))],
        compiler_params=pltpu.CompilerParams(collective_id=0, has_side_effects=True),
    )(panel)


def local(data, impulse, wavelet, live):
    rows_dev = data.shape[2]
    shots_dev = data.shape[3]
    positions = impulse.shape[3]
    groups = lax.axis_size("shot")
    total_shots = shots_dev * groups
    spacing = positions // total_shots
    scale = -(total_shots ** (-0.5))
    j = lax.axis_index("shot")
    mask = live.astype(jnp.float32)
    observed = data[0] * mask[None]
    row_ids = lax.axis_index("rcv") * rows_dev + lax.broadcasted_iota(jnp.int32, (rows_dev, shots_dev), 0)
    col_ids = j * shots_dev + lax.broadcasted_iota(jnp.int32, (rows_dev, shots_dev), 1)
    source = (row_ids == col_ids * spacing).astype(jnp.float32)
    panel = wavelet[0][:, None, None] * source[None] - observed
    if lax.axis_size("rcv") == 2 * groups:
        part = spread(panel, groups)
    else:
        whole = lax.all_gather(panel, "rcv", axis=1, tiled=True)
        part = lax.all_to_all(whole, "shot", split_axis=1, concat_axis=2, tiled=True)
    quarter = positions // groups
    imp = lax.dynamic_slice_in_dim(impulse[0], j * quarter, quarter, axis=2)
    predicted = lax.psum_scatter(convolve(imp, part), "shot", scatter_dimension=2, tiled=True)
    residual = mask[None] * (observed - predicted)
    every = lax.all_gather(residual, "shot", axis=2, tiled=True)
    gradient = correlate(every, part, scale)
    return (residual[None], gradient[None])


def solution(mesh):
    placed = (P(None, None, "rcv", "shot"), P(None, None, "rcv", None), P(), P("rcv", "shot"))
    return jax.shard_map(
        local,
        mesh=mesh,
        in_specs=placed,
        out_specs=(P(None, None, "rcv", "shot"), P(None, None, "rcv", "shot")),
        check_vma=False,
    )
```

time: 1020 us -> 610 us (0.60)
  waiting for transfers between devices: 679 us -> 190 us
  Pallas kernels: 0 us -> 215 us
  matrix products: 262 us -> 152 us
  other arithmetic: 49 us -> 28.5 us
    reduce_scatter x1, waiting for transfers between devices: 449 us -> 132 us  [local(): lax.psum_scatter(convolve(imp, part), 'shot', scatter_dimension=2, tiled=...]
    pallas_call x0 -> x1, Pallas kernels: none -> 215 us  [spread(): pl.pallas_call(functools.partial(spread_kernel, planes), out_shape=jax.Sh...]
    all_gather x1, waiting for transfers between devices: 230 us -> 58.4 us  [local(): every = lax.all_gather(residual, 'shot', axis=2, tiled=True)]
    dot_general x8, matrix products: 262 us -> 152 us  [product(): jnp.einsum(form, left, right, precision=PRECISION, preferred_element_type...]
    mul x2, other arithmetic: 44.9 us -> 15.2 us  [the longest x1 12 us: correlate(): return jnp.stack([out_re, out_im]) * scale]
where the time goes in v1:
time: 610 us; the launch traced here: 601 us
  Pallas kernels  215 us (35%)
  waiting for transfers between devices  190 us (31%)
  matrix products  152 us (25%)
  other arithmetic  28.5 us (5%)
  between operations  14.6 us (2%)
    pallas_call x1, Pallas kernels, spread(): pl.pallas_call(functools.partial(spread_kernel, planes), out_shape=jax.Sh...  215 us
    dot_general x8, matrix products, product(): jnp.einsum(form, left, right, precision=PRECISION, preferred_element_type...  152 us
    reduce_scatter x1, waiting for transfers between devices, local(): lax.psum_scatter(convolve(imp, part), 'shot', scatter_dimension=2, tiled=...  132 us
    all_gather x1, waiting for transfers between devices, local(): every = lax.all_gather(residual, 'shot', axis=2, tiled=True)  58.4 us
  transfers between devices with their start and end apart: 2, of which 2 were waited for; matrix products, arithmetic and copies ran while one was open for 0% of the time, Pallas kernels for 0%

profile of v1, /device:TPU:0, one launch (start us, length us, event | category | flops | bytes accessed | tf_op | source)
XLA Modules:
  0.0 600.6 jit_solution(6510187961938197783)
XLA Ops:
  7.2 0.0 reduce-scatter.2.cloned.1.call-start
  7.2 1.3 convert_element_type.10
  8.5 0.2 compare_convert_fusion
  8.8 3.2 multiply_subtract_fusion.panel_ref
  12.0 215.2 %shard_map.59 = f32[2,2048,1024]{2,1,0:T(8,128)} custom-call(f32[2,1024,256]{2,1,0:T(8,128)} %multiply_subtract_fusion.panel_ref), custom_call_target="tpu_custom_call" | custom-call | tf_op jit(solution)/shard_map/pallas_call | solution.py:143
  227.2 0.0 copy-start
  227.2 19.5 %fusion.4 = f32[1024,1024]{1,0:T(8,128)} fusion(f32[1,2,1024,8192]{3,2,1,0:T(8,128)} %param.5, s32[]{:T(128)S(6)} %select_n.3, f32[2,2048,1024]{2,1,0:T(8,128)} %shard_map.59), kind=kOutput, calls=%fused_computation.8 | convolution fusion | flops 12884901888 | bytes 20971524 | tf_op jit(solution)/shard_map/rk,ks->rs/dot_general | solution.py:15
  246.7 0.0 copy-done
  246.7 18.3 %fusion.6 = f32[1024,1024]{1,0:T(8,128)} fusion(f32[1,2,1024,8192]{3,2,1,0:T(8,128)} %param.5, s32[]{:T(128)S(6)} %add.32, s32[]{:T(128)S(6)} %select_n.3, f32[2,2048,1024]{2,1,0:T(8,128)S(1)} %copy-done), kind=kOutput, calls=%fused_computation.10 | convolution fusion | flops 12884901888 | bytes 20971528 | tf_op jit(solution)/shard_map/rk,ks->rs/dot_general | solution.py:15
  265.1 20.3 %add_bitcast_fusion.1 = f32[1,1024,1024]{2,1,0:T(8,128)} fusion(f32[1024,1024]{1,0:T(8,128)} %fusion.4, f32[2,2048,1024]{2,1,0:T(8,128)S(1)} %copy-done, f32[1,2,1024,8192]{3,2,1,0:T(8,128)} %param.5, s32[]{:T(128)S(6)} %add.32, s32[]{:T(128)S(6)} %select_n.3), kind=kOutput, calls=%fused_computation.32 | convolution fusion | flops 12885950464 | bytes 25165832 | tf_op jit(solution)/shard_map/rk,ks->rs/dot_general | solution.py:15
  285.4 20.2 %subtract_bitcast_fusion.1 = f32[1,1024,1024]{2,1,0:T(8,128)} fusion(f32[1024,1024]{1,0:T(8,128)} %fusion.6, f32[2,2048,1024]{2,1,0:T(8,128)S(1)} %copy-done, f32[1,2,1024,8192]{3,2,1,0:T(8,128)} %param.5, s32[]{:T(128)S(6)} %select_n.3), kind=kOutput, calls=%fused_computation.33 | convolution fusion | flops 12885950464 | bytes 25165828 | tf_op jit(solution)/shard_map/rk,ks->rs/dot_general | solution.py:15
  305.5 8.5 %pad_maximum_fusion = f32[2,1024,1024]{2,1,0:T(8,128)} fusion(f32[1,1024,1024]{2,1,0:T(8,128)} %add_bitcast_fusion.1, f32[1,1024,1024]{2,1,0:T(8,128)} %subtract_bitcast_fusion.1), kind=kLoop, calls=%fused_computation.3 | loop fusion | flops 2097152 | bytes 16777216 | tf_op jit(solution)/shard_map/stack | solution.py:22
  314.1 0.0 reduce-scatter.2.cloned.1.call-update
  314.1 0.0 all-gather.2.cloned.1.call-start
  314.1 131.7 %reduce-scatter.2.cloned.1.call-done = f32[2,1024,256]{2,1,0:T(8,128)} async-done(((f32[2,1024,1024]{2,1,0:T(8,128)}), f32[2,1024,256]{2,1,0:T(8,128)}) %reduce-scatter.2.cloned.1.call-update) | async-done | bytes 2097168 | tf_op jit(solution)/shard_map/reduce_scatter | solution.py:176
  445.9 3.2 subtract_multiply_fusion
  449.1 0.0 all-gather.2.cloned.1.call-update
  449.1 58.4 %all-gather.2.cloned.1.call-done = f32[2,1024,1024]{2,1,0:T(8,128)} async-done(((f32[2,1024,256]{2,1,0:T(8,128)}), f32[2,1024,1024]{2,1,0:T(8,128)}) %all-gather.2.cloned.1.call-update) | async-done | bytes 8388624 | tf_op jit(solution)/shard_map/all_gather | solution.py:178
  507.6 18.7 %fusion = f32[1024,2048]{1,0:T(8,128)} fusion(f32[2,2048,1024]{2,1,0:T(8,128)} %shard_map.59, f32[2,1024,1024]{2,1,0:T(8,128)} %all-gather.2.cloned.1.call-done), kind=kOutput, calls=%fused_computation.4 | convolution fusion | flops 12884901888 | bytes 20971520 | tf_op jit(solution)/shard_map/rs,ks->rk/dot_general | solution.py:15
  526.3 17.1 %fusion.2 = f32[1024,2048]{1,0:T(8,128)} fusion(f32[2,2048,1024]{2,1,0:T(8,128)} %shard_map.59, f32[2,1024,1024]{2,1,0:T(8,128)S(1)} %copy-done.2), kind=kOutput, calls=%fused_computation.6 | convolution fusion | flops 12884901888 | bytes 20971520 | tf_op jit(solution)/shard_map/rs,ks->rk/dot_general | solution.py:15
  543.4 0.0 slice-done.1
  543.4 18.8 %subtract_bitcast_fusion = f32[1,1,1024,2048]{3,2,1,0:T(8,128)} fusion(f32[1024,2048]{1,0:T(8,128)} %fusion, f32[2,2048,1024]{2,1,0:T(8,128)S(1)} %bitcast.67, f32[2,1024,1024]{2,1,0:T(8,128)} %all-gather.2.cloned.1.call-done), kind=kOutput, calls=%fused_computation.20 | convolution fusion | flops 12886999040 | bytes 29360128 | tf_op jit(solution)/shard_map/rs,ks->rk/dot_general | solution.py:15
  562.3 19.0 %add_bitcast_fusion = f32[1,1,1024,2048]{3,2,1,0:T(8,128)} fusion(f32[1024,2048]{1,0:T(8,128)} %fusion.2, f32[2,2048,1024]{2,1,0:T(8,128)S(1)} %bitcast.67, f32[2,1024,1024]{2,1,0:T(8,128)} %all-gather.2.cloned.1.call-done), kind=kOutput, calls=%fused_computation.21 | convolution fusion | flops 12886999040 | bytes 29360128 | tf_op jit(solution)/shard_map/rs,ks->rk/dot_general | solution.py:15
  581.3 12.0 %maximum_multiply_fusion = f32[1,2,1024,2048]{3,2,1,0:T(8,128)} fusion(f32[1,1,1024,2048]{3,2,1,0:T(8,128)} %subtract_bitcast_fusion, f32[1,1,1024,2048]{3,2,1,0:T(8,128)} %add_bitcast_fusion), kind=kLoop, calls=%fused_computation | loop fusion | flops 8388608 | bytes 33554432 | tf_op jit(solution)/shard_map/mul | solution.py:29
  (14 shorter events, 0.0 us)
Async XLA Ops:
  7.2 438.7 %reduce-scatter.2.cloned.1.call-start = ((), (), s32[]{:S(2)}) async-start(), calls=%async_computation.1 | async-start | bytes 10485760 | tf_op jit(solution)/shard_map/reduce_scatter | solution.py:176
  227.2 19.5 %copy-start = (f32[2,2048,1024]{2,1,0:T(8,128)S(1)}, f32[2,2048,1024]{2,1,0:T(8,128)}, u32[]{:S(2)}) copy-start(f32[2,2048,1024]{2,1,0:T(8,128)} %shard_map.59) | copy-start | bytes 50331652
  314.1 131.8 %copy-start.1 = (f32[1,2,1024,256]{3,2,1,0:T(8,128)S(1)}, f32[1,2,1024,256]{3,2,1,0:T(8,128)}, u32[]{:S(2)}) copy-start(f32[1,2,1024,256]{3,2,1,0:T(8,128)} %param.4) | copy-start | bytes 6291460
  314.1 193.5 %all-gather.2.cloned.1.call-start = ((), (), s32[]{:S(2)}) async-start(), calls=%async_computation.2 | async-start | bytes 10485760 | tf_op jit(solution)/shard_map/all_gather | solution.py:178
  507.6 18.7 %copy-start.2 = (f32[2,1024,1024]{2,1,0:T(8,128)S(1)}, f32[2,1024,1024]{2,1,0:T(8,128)}, u32[]{:S(2)}) copy-start(f32[2,1024,1024]{2,1,0:T(8,128)} %all-gather.2.cloned.1.call-done) | copy-start | bytes 25165828
  507.6 35.8 %slice-start = ((s8[16777216]{0:T(1024)(128)(4,1)}), s8[4194304]{0:T(1024)(128)(4,1)S(1)}, s32[]{:S(2)}) async-start(s8[16777216]{0:T(1024)(128)(4,1)} %bitcast.66), calls=%async_computation.3 | async-start | bytes 8388608
  507.6 35.8 %slice-start.1 = ((s8[16777216]{0:T(1024)(128)(4,1)}), s8[4194304]{0:T(1024)(128)(4,1)S(1)}, s32[]{:S(2)}) async-start(s8[16777216]{0:T(1024)(128)(4,1)} %bitcast.66), calls=%async_computation.4 | async-start | bytes 8388608
  526.3 17.1 %slice-start.2 = ((s8[16777216]{0:T(1024)(128)(4,1)}), s8[4194304]{0:T(1024)(128)(4,1)S(1)}, s32[]{:S(2)}) async-start(s8[16777216]{0:T(1024)(128)(4,1)} %bitcast.66), calls=%async_computation.5 | async-start | bytes 8388608
  526.3 17.1 %slice-start.3 = ((s8[16777216]{0:T(1024)(128)(4,1)}), s8[4194304]{0:T(1024)(128)(4,1)S(1)}, s32[]{:S(2)}) async-start(s8[16777216]{0:T(1024)(128)(4,1)} %bitcast.66), calls=%async_computation.6 | async-start | bytes 8388608
Sparse Core Ops, SparseCore 0:
  314.2 131.6 reduce-scatter.1
  449.3 58.2 all-gather.1
